TPU v7x, 32 devices: a whole 2x2x4 slice. The times are simulated.
32 devices in a mesh: groups: 2 (over x), tile: 16 (over z, y, core).
Axes of the slice: x: 2, y: 2, z: 4, core: 2. Of those that a mesh axis runs over, the one named last changes fastest.
Arguments:
- observations: bfloat16 [2048, 64, 256], P(('groups', 'tile')), parts along dimension 0, may hold values from -6 to 6
- pixel_geometry: float32 [2048, 8, 256], P(('groups', 'tile')), parts along dimension 0, as said below
- block_counts: int32 [2048], P(('groups', 'tile')), parts along dimension 0, may hold values from 1 to 256, as said below
- block_tiles: int32 [2048], P(('groups', 'tile')), parts along dimension 0, may hold values from 0 to 511, as said below
- cutoff_lists: int32 [512, 3], replicated, may hold values from 0 to 127, as said below
- patch_geometry: float32 [4, 32768], replicated, as said below
- stress: bfloat16 [64, 65536], P(None, ('groups', 'tile')), parts along dimension 1, may hold values from -3 to 3
- screens: bfloat16 [1024, 64, 256], P(('groups', 'tile')), parts along dimension 0, may hold values from -3 to 3
Outputs:
- stress_gradient: float32 [64, 65536], P(None, ('groups', 'tile')), parts along dimension 1
- screen_gradient: float32 [1024, 64, 256], P(('groups', 'tile')), parts along dimension 0
There are 2 independent parts, one for each index of `groups`. A program takes and returns all parts, laid end to end along the dimension named above; an argument that names none is the same for every part. Nothing has to cross between parts.
Inputs may be any that keep to these rules, and one draw needn't show every extreme that they name: `block_tiles`: the owner of tile t is index t // 32 of tile. Among the 64 blocks of one device at most 8 belong to the tiles of one owner, and some owner gets exactly 8 from every device. The live pixels of a block are its first block_counts pixels. `cutoff_lists`: the 3 entries of a row are different patch blocks. `patch_geometry`: depths are 1 or more; compliances are positive. `pixel_geometry`: u and v lie within 0 to 15; weights are positive.
All inputs are finite; a program needn't handle non-finite values.
Results may differ from a plain program's by a relative error of at most 0.0037.
Values may be sent and summed in bfloat16 or wider, within the bound.
No kernel may reach another device: no remote copies, remote signals or barrier semaphores. Data moves between devices by JAX's collectives and lax.ppermute only.
A program may use at most 128 MiB of HBM per device.

v0:
```python
import jax
import jax.numpy as jnp
from jax import lax
from jax.sharding import PartitionSpec as P

PBLK = 256
NEAR = 3
SG = 16


def green_block(pixels, patches):
    east = pixels[0][:, None] - patches[0][None, :]
    north = pixels[1][:, None] - patches[1][None, :]
    depth = patches[2][None, :]
    radius = east * east + north * north + depth * depth
    inverse = lax.rsqrt(radius)
    along = pixels[4][:, None] * east + pixels[5][:, None] * north + pixels[6][:, None] * depth
    return (patches[3][None, :] * depth * depth * along * inverse * inverse * inverse).astype(
        jnp.bfloat16
    )


def hat_block(pixels, nodes):
    grid = jnp.arange(nodes).astype(jnp.float32)
    across = jnp.maximum(0.0, 1.0 - jnp.abs(pixels[2][:, None] - grid[None, :]))
    upward = jnp.maximum(0.0, 1.0 - jnp.abs(pixels[3][:, None] - grid[None, :]))
    return (
        (across[:, :, None] * upward[:, None, :])
        .reshape(pixels.shape[1], nodes * nodes)
        .astype(jnp.bfloat16)
    )


def near_pieces(tile, cutoff_lists, patch_blocks, stress_blocks):
    near = cutoff_lists[tile]
    patches = patch_blocks[:, near].reshape(patch_blocks.shape[0], -1)
    stress_near = stress_blocks[:, near].reshape(stress_blocks.shape[0], -1)
    return (near, patches, stress_near)


def predict(green, stress_near):
    return lax.dot_general(
        stress_near, green, (((1,), (1,)), ((), ())), preferred_element_type=jnp.float32
    )


def weigh(prediction, screen, hats, observed, pixels, count):
    correction = lax.dot_general(
        screen, hats, (((1,), (1,)), ((), ())), preferred_element_type=jnp.float32
    )
    live = jnp.arange(pixels.shape[1]) < count
    scale = jnp.where(live, pixels[7], 0.0)
    return ((prediction + correction - observed.astype(jnp.float32)) * scale[None, :]).astype(
        jnp.bfloat16
    )


def add_terms(grad, near, terms):
    epochs = terms.shape[1]
    flat = jnp.moveaxis(terms, 0, 1).reshape(epochs, near.shape[0] * near.shape[1], PBLK)
    return grad.at[:, near.reshape(-1)].add(flat)


def grouped(arrays, total):
    return tuple((item.reshape((16, total // 16) + item.shape[1:]) for item in arrays))


def on_device(
    observations,
    pixel_geometry,
    block_counts,
    block_tiles,
    cutoff_lists,
    patch_geometry,
    stress,
    screens,
):
    devices = lax.axis_size("tile")
    here = lax.axis_index("tile")
    local_tiles = screens.shape[0]
    blocks = observations.shape[0]
    epochs = observations.shape[1]
    width = observations.shape[2]
    slots_each = 2 * blocks // devices
    slots = devices * slots_each
    full = lax.all_gather(stress, "tile", axis=1, tiled=True)
    patch_count = full.shape[1]
    stress_blocks = full.reshape(epochs, patch_count // PBLK, PBLK)
    patch_blocks = patch_geometry.reshape(4, patch_count // PBLK, PBLK)
    owners = block_tiles // local_tiles
    same = owners[:, None] == owners[None, :]
    earlier = jnp.arange(blocks)[:, None] > jnp.arange(blocks)[None, :]
    rank = jnp.sum(jnp.logical_and(same, earlier), axis=1)
    place = owners * slots_each + rank
    meta = jnp.stack([block_counts, block_tiles], axis=1)

    def packed(values):
        empty = jnp.zeros((slots,) + values.shape[1:], values.dtype)
        return empty.at[place].set(values).reshape((devices, slots_each) + values.shape[1:])

    def local_of(tile):
        return jnp.clip(tile - here * local_tiles, 0, local_tiles - 1)

    got_obs = lax.all_to_all(
        packed(observations), "tile", split_axis=0, concat_axis=0, tiled=True
    ).reshape((slots, epochs, width))
    start_grad = jnp.zeros((epochs, patch_count // PBLK, PBLK), jnp.float32)
    start_screen = jnp.zeros(screens.shape, jnp.float32)
    got_pix, got_meta = (
        lax.all_to_all(packed(pixel_geometry), "tile", split_axis=0, concat_axis=0, tiled=True),
        lax.all_to_all(packed(meta), "tile", split_axis=0, concat_axis=0, tiled=True),
    )
    got_pix = got_pix.reshape((slots, 8, width))
    got_meta = got_meta.reshape((slots, 2))

    def one(observed, pixels, info):
        near, patches, stress_near = near_pieces(info[1], cutoff_lists, patch_blocks, stress_blocks)
        green = green_block(pixels, patches)
        hats = hat_block(pixels, SG)
        local = local_of(info[1])
        weighted = weigh(
            predict(green, stress_near), screens[local], hats, observed, pixels, info[0]
        )
        terms = jnp.dot(weighted, green, preferred_element_type=jnp.float32).reshape(
            epochs, NEAR, PBLK
        )
        return (near, terms, local, jnp.dot(weighted, hats, preferred_element_type=jnp.float32))

    def step(state, pieces):
        grad, screen_grad = state
        near, terms, local, screen_terms = jax.vmap(one)(*pieces)
        return ((add_terms(grad, near, terms), screen_grad.at[local].add(screen_terms)), None)

    grad, screen_gradient = lax.scan(
        step, (start_grad, start_screen), grouped((got_obs, got_pix, got_meta), slots)
    )[0]
    stress_gradient = lax.psum_scatter(
        grad.reshape((epochs, patch_count)), "tile", scatter_dimension=1, tiled=True
    )
    return (stress_gradient, screen_gradient)


def solution(mesh):
    return jax.shard_map(
        on_device,
        mesh=mesh,
        in_specs=(
            P(("groups", "tile"), None, None),
            P(("groups", "tile"), None, None),
            P(("groups", "tile")),
            P(("groups", "tile")),
            P(),
            P(),
            P(None, ("groups", "tile")),
            P(("groups", "tile"), None, None),
        ),
        out_specs=(P(None, ("groups", "tile")), P(("groups", "tile"), None, None)),
        check_vma=False,
    )
```

profile of v0, /device:TPU:0, one launch (start us, length us, event | category | flops | bytes accessed | tf_op | source)
XLA Modules:
  0.0 850.3 jit_solution(3654755080954400022)
XLA Ops:
  11.1 7.4 all-to-all-start
  19.6 8.0 scatter_fusion.2
  36.8 8.7 %scatter_fusion.3 = bf16[128,64,256]{2,1,0:T(8,128)(2,1)} fusion(bf16[128,64,256]{2,1,0:T(8,128)(2,1)} %broadcast_in_dim.20, s32[64]{0:T(128)S(1)} %compare_select_fusion.4, bf16[64,64,256]{2,1,0:T(8,128)(2,1)S(1)} %copy-done), kind=kCustom, calls=%fused_computation.8 | custom fusion | bytes 6291712 | tf_op jit(solution)/shard_map/scatter | solution.py:99
  45.5 16.1 %all-to-all-done.1 = f32[16,8,8,256]{3,2,1,0:T(8,128)S(1)} async-done(((f32[16,8,8,256]{3,2,1,0:T(8,128)}), f32[16,8,8,256]{3,2,1,0:T(8,128)S(1)}, u32[]{:S(2)}, u32[]{:S(2)}) %all-to-all-start.1) | async-done | bytes 1048608 | tf_op jit(solution)/shard_map/all_to_all | solution.py:110
  61.6 10.3 %all-to-all-start.2 = ((bf16[16,8,64,256]{3,2,1,0:T(8,128)(2,1)}), bf16[16,8,64,256]{3,2,1,0:T(8,128)(2,1)}, u32[]{:S(2)}, u32[]{:S(2)}) async-start(bf16[16,8,64,256]{3,2,1,0:T(8,128)(2,1)} %bitcast.132), calls=%async_computation.2 | async-start | bytes 8388608 | tf_op jit(solution)/shard_map/all_to_all | solution.py:104
  72.1 50.8 %all-gather.2.cloned.1.call-done = bf16[64,32768]{1,0:T(8,128)(2,1)} async-done(((bf16[64,2048]{1,0:T(8,128)(2,1)}), bf16[64,32768]{1,0:T(8,128)(2,1)}) %all-gather.2.cloned.1.call-update) | async-done | bytes 4194320 | tf_op jit(solution)/shard_map/all_gather | solution.py:86
  127.6 37.3 %all-to-all-done.2 = bf16[16,8,64,256]{3,2,1,0:T(8,128)(2,1)} async-done(((bf16[16,8,64,256]{3,2,1,0:T(8,128)(2,1)}), bf16[16,8,64,256]{3,2,1,0:T(8,128)(2,1)}, u32[]{:S(2)}, u32[]{:S(2)}) %all-to-all-start.2) | async-done | bytes 4194336 | tf_op jit(solution)/shard_map/all_to_all | solution.py:104
  170.7 543.8 %while.14 = (s32[]{:T(128)}, f32[64,128,256]{2,0,1:T(8,128)}, f32[32,64,256]{2,1,0:T(8,128)}, s32[16,8,2]{1,2,0:T(2,128)S(1)}, s32[512,3]{1,0:T(8,128)S(1)}, /*i...) while((s32[]{:T(128)}, f32[64,128,256]{2,0,1:T(8,128)}, ...), condition=%wide.region_7.8_spmd, body=%wide.region_4.7_spmd.sunk | while | flops 589716736 | bytes 35117604 | solution.py:134
  198.2 6.5 scatter_fusion
  232.2 6.5 scatter_fusion
  266.2 6.5 scatter_fusion
  300.2 6.5 scatter_fusion
  334.2 6.5 scatter_fusion
  368.2 6.5 scatter_fusion
  402.2 6.5 scatter_fusion
  436.1 6.5 scatter_fusion
  470.1 6.5 scatter_fusion
  504.1 6.5 scatter_fusion
  538.1 6.5 scatter_fusion
  572.1 6.5 scatter_fusion
  640.1 6.5 scatter_fusion
  708.1 6.5 scatter_fusion
  714.6 7.4 copy.77
  722.0 121.4 %reduce-scatter.2.cloned.1.call-done = f32[64,2048]{1,0:T(8,128)} async-done(((f32[64,32768]{1,0:T(8,128)}), f32[64,2048]{1,0:T(8,128)}) %reduce-scatter.2.cloned.1.call-update) | async-done | bytes 524304 | tf_op jit(solution)/shard_map/reduce_scatter | solution.py:137
  (569 shorter events, 475.6 us)
Async XLA Ops:
  7.2 29.6 %copy-start = (bf16[64,64,256]{2,1,0:T(8,128)(2,1)S(1)}, bf16[64,64,256]{2,1,0:T(8,128)(2,1)}, u32[]{:S(2)}) copy-start(bf16[64,64,256]{2,1,0:T(8,128)(2,1)} %param.10) | copy-start | bytes 6291460
  11.1 16.4 %all-to-all-start = ((s32[16,8,2]{1,2,0:T(2,128)}), s32[16,8,2]{1,2,0:T(2,128)S(1)}, u32[]{:S(2)}, u32[]{:S(2)}) async-start(s32[16,8,2]{1,2,0:T(2,128)} %copy.65), calls=%async_computation | async-start | bytes 32768 | tf_op jit(solution)/shard_map/all_to_all | solution.py:111
  27.5 34.0 %all-to-all-start.1 = ((f32[16,8,8,256]{3,2,1,0:T(8,128)}), f32[16,8,8,256]{3,2,1,0:T(8,128)S(1)}, u32[]{:S(2)}, u32[]{:S(2)}) async-start(f32[16,8,8,256]{3,2,1,0:T(8,128)} %bitcast.34), calls=%async_computation.1 | async-start | bytes 2097152 | tf_op jit(solution)/shard_map/all_to_all | solution.py:110
  33.6 89.3 %all-gather.2.cloned.1.call-start = ((), (), s32[]{:S(2)}) async-start(), calls=%async_computation.4 | async-start | bytes 4456448 | tf_op jit(solution)/shard_map/all_gather | solution.py:86
  36.8 35.1 %copy-start.3 = (s32[512,3]{0,1:T(4,128)S(1)}, s32[512,3]{0,1:T(4,128)}, u32[]{:S(2)}) copy-start(s32[512,3]{0,1:T(4,128)} %param.14) | copy-start | bytes 18436
  61.6 103.3 %all-to-all-start.2 = ((bf16[16,8,64,256]{3,2,1,0:T(8,128)(2,1)}), bf16[16,8,64,256]{3,2,1,0:T(8,128)(2,1)}, u32[]{:S(2)}, u32[]{:S(2)}) async-start(bf16[16,8,64,256]{3,2,1,0:T(8,128)(2,1)} %bitcast.132), calls=%async_computation.2 | async-start | bytes 8388608 | tf_op jit(solution)/shard_map/all_to_all | solution.py:104
  71.9 771.6 %reduce-scatter.2.cloned.1.call-start = ((), (), s32[]{:S(2)}) async-start(), calls=%async_computation.5 | async-start | bytes 8912896 | tf_op jit(solution)/shard_map/reduce_scatter | solution.py:137
  170.7 13.1 %copy-start.1 = (f32[16,8,8,256]{3,2,1,0:T(8,128)}, f32[16,8,8,256]{3,2,1,0:T(8,128)S(1)}, u32[]{:S(2)}) copy-start(f32[16,8,8,256]{3,2,1,0:T(8,128)S(1)} %get-tuple-element.366) | copy-start | bytes 3145732 | tf_op jit(solution)/shard_map/while
  195.4 9.3 %copy-start.2 = (f32[16,8,8,256]{3,2,1,0:T(8,128)S(1)}, f32[16,8,8,256]{3,2,1,0:T(8,128)}, u32[]{:S(2)}) copy-start(f32[16,8,8,256]{3,2,1,0:T(8,128)} %copy-done.1) | copy-start | bytes 3145732 | tf_op jit(solution)/shard_map/while
  204.7 13.1 %copy-start.1 = (f32[16,8,8,256]{3,2,1,0:T(8,128)}, f32[16,8,8,256]{3,2,1,0:T(8,128)S(1)}, u32[]{:S(2)}) copy-start(f32[16,8,8,256]{3,2,1,0:T(8,128)S(1)} %get-tuple-element.366) | copy-start | bytes 3145732 | tf_op jit(solution)/shard_map/while
  238.7 13.1 %copy-start.1 = (f32[16,8,8,256]{3,2,1,0:T(8,128)}, f32[16,8,8,256]{3,2,1,0:T(8,128)S(1)}, u32[]{:S(2)}) copy-start(f32[16,8,8,256]{3,2,1,0:T(8,128)S(1)} %get-tuple-element.366) | copy-start | bytes 3145732 | tf_op jit(solution)/shard_map/while
  272.7 13.1 %copy-start.1 = (f32[16,8,8,256]{3,2,1,0:T(8,128)}, f32[16,8,8,256]{3,2,1,0:T(8,128)S(1)}, u32[]{:S(2)}) copy-start(f32[16,8,8,256]{3,2,1,0:T(8,128)S(1)} %get-tuple-element.366) | copy-start | bytes 3145732 | tf_op jit(solution)/shard_map/while
  306.7 13.1 %copy-start.1 = (f32[16,8,8,256]{3,2,1,0:T(8,128)}, f32[16,8,8,256]{3,2,1,0:T(8,128)S(1)}, u32[]{:S(2)}) copy-start(f32[16,8,8,256]{3,2,1,0:T(8,128)S(1)} %get-tuple-element.366) | copy-start | bytes 3145732 | tf_op jit(solution)/shard_map/while
  340.7 13.1 %copy-start.1 = (f32[16,8,8,256]{3,2,1,0:T(8,128)}, f32[16,8,8,256]{3,2,1,0:T(8,128)S(1)}, u32[]{:S(2)}) copy-start(f32[16,8,8,256]{3,2,1,0:T(8,128)S(1)} %get-tuple-element.366) | copy-start | bytes 3145732 | tf_op jit(solution)/shard_map/while
  374.7 13.1 %copy-start.1 = (f32[16,8,8,256]{3,2,1,0:T(8,128)}, f32[16,8,8,256]{3,2,1,0:T(8,128)S(1)}, u32[]{:S(2)}) copy-start(f32[16,8,8,256]{3,2,1,0:T(8,128)S(1)} %get-tuple-element.366) | copy-start | bytes 3145732 | tf_op jit(solution)/shard_map/while
  408.7 13.1 %copy-start.1 = (f32[16,8,8,256]{3,2,1,0:T(8,128)}, f32[16,8,8,256]{3,2,1,0:T(8,128)S(1)}, u32[]{:S(2)}) copy-start(f32[16,8,8,256]{3,2,1,0:T(8,128)S(1)} %get-tuple-element.366) | copy-start | bytes 3145732 | tf_op jit(solution)/shard_map/while
  442.6 13.1 %copy-start.1 = (f32[16,8,8,256]{3,2,1,0:T(8,128)}, f32[16,8,8,256]{3,2,1,0:T(8,128)S(1)}, u32[]{:S(2)}) copy-start(f32[16,8,8,256]{3,2,1,0:T(8,128)S(1)} %get-tuple-element.366) | copy-start | bytes 3145732 | tf_op jit(solution)/shard_map/while
  476.6 13.1 %copy-start.1 = (f32[16,8,8,256]{3,2,1,0:T(8,128)}, f32[16,8,8,256]{3,2,1,0:T(8,128)S(1)}, u32[]{:S(2)}) copy-start(f32[16,8,8,256]{3,2,1,0:T(8,128)S(1)} %get-tuple-element.366) | copy-start | bytes 3145732 | tf_op jit(solution)/shard_map/while
  510.6 13.1 %copy-start.1 = (f32[16,8,8,256]{3,2,1,0:T(8,128)}, f32[16,8,8,256]{3,2,1,0:T(8,128)S(1)}, u32[]{:S(2)}) copy-start(f32[16,8,8,256]{3,2,1,0:T(8,128)S(1)} %get-tuple-element.366) | copy-start | bytes 3145732 | tf_op jit(solution)/shard_map/while
  544.6 13.1 %copy-start.1 = (f32[16,8,8,256]{3,2,1,0:T(8,128)}, f32[16,8,8,256]{3,2,1,0:T(8,128)S(1)}, u32[]{:S(2)}) copy-start(f32[16,8,8,256]{3,2,1,0:T(8,128)S(1)} %get-tuple-element.366) | copy-start | bytes 3145732 | tf_op jit(solution)/shard_map/while
  578.6 13.1 %copy-start.1 = (f32[16,8,8,256]{3,2,1,0:T(8,128)}, f32[16,8,8,256]{3,2,1,0:T(8,128)S(1)}, u32[]{:S(2)}) copy-start(f32[16,8,8,256]{3,2,1,0:T(8,128)S(1)} %get-tuple-element.366) | copy-start | bytes 3145732 | tf_op jit(solution)/shard_map/while
  612.6 13.1 %copy-start.1 = (f32[16,8,8,256]{3,2,1,0:T(8,128)}, f32[16,8,8,256]{3,2,1,0:T(8,128)S(1)}, u32[]{:S(2)}) copy-start(f32[16,8,8,256]{3,2,1,0:T(8,128)S(1)} %get-tuple-element.366) | copy-start | bytes 3145732 | tf_op jit(solution)/shard_map/while
  646.6 13.1 %copy-start.1 = (f32[16,8,8,256]{3,2,1,0:T(8,128)}, f32[16,8,8,256]{3,2,1,0:T(8,128)S(1)}, u32[]{:S(2)}) copy-start(f32[16,8,8,256]{3,2,1,0:T(8,128)S(1)} %get-tuple-element.366) | copy-start | bytes 3145732 | tf_op jit(solution)/shard_map/while
  680.6 13.1 %copy-start.1 = (f32[16,8,8,256]{3,2,1,0:T(8,128)}, f32[16,8,8,256]{3,2,1,0:T(8,128)S(1)}, u32[]{:S(2)}) copy-start(f32[16,8,8,256]{3,2,1,0:T(8,128)S(1)} %get-tuple-element.366) | copy-start | bytes 3145732 | tf_op jit(solution)/shard_map/while
  (15 other events, 139.2 us)
Sparse Core Ops, SparseCore 0:
  36.6 86.2 all-gather.1
  722.1 121.2 reduce-scatter.1
where the time goes:
time: 857 us; the launch traced here: 850 us
  waiting for transfers between devices  226 us (26%)
  local copies, waits for them, and re-layouts  222 us (26%)
  matrix products  201 us (23%)
  other arithmetic  160 us (19%)
  starting transfers between devices  23.8 us (3%)
  between operations  14.1 us (2%)
    reduce_scatter x1, waiting for transfers between devices, on_device(): lax.psum_scatter(grad.reshape((epochs, patch_count)), 'tile', scatter_dim...  121 us
    scatter-add x16, other arithmetic, add_terms(): return grad.at[:, near.reshape(-1)].add(flat)  104 us
    dot_general x16, matrix products, one(): jnp.dot(weighted, green, preferred_element_type=jnp.float32)  87.7 us
    dot_general x16, matrix products, predict(): lax.dot_general(stress_near, green, (((1,), (1,)), ((), ())), preferred_e...  86.6 us
    all_gather x1, waiting for transfers between devices, on_device(): full = lax.all_gather(stress, 'tile', axis=1, tiled=True)  50.8 us
    gather x16, local copies, waits for them, and re-layouts, near_pieces(): stress_near = stress_blocks[:, near].reshape(stress_blocks.shape[0], -1)  44.6 us
    scatter-add x16, other arithmetic, step(): screen_grad.at[local].add(screen_terms)  44.4 us
    reshape x16, local copies, waits for them, and re-layouts, one(): jnp.dot(weighted, green, preferred_element_type=jnp.float32)  41.8 us
  transfers between devices with their start and end apart: 5, of which 4 were waited for; matrix products, arithmetic and copies ran while one was open for 3% of the time, Pallas kernels for 0%

commit v1 on v0

v1 whole, which is shorter than its diff:
```python
import functools

import jax
import jax.numpy as jnp
from jax import lax
from jax.experimental import pallas as pl
from jax.experimental.pallas import tpu as pltpu
from jax.sharding import PartitionSpec as P

PBLK = 256
NEAR = 3
SG = 16
CHUNK = 128
PARTS = 2
NARROW = 3
MIB = 1 << 20


def pack_kernel(local_tiles, parts, each, tiles, counts, obs, pix, *rest):
    obs_out, pix_out = rest[:parts], rest[parts : 2 * parts]
    meta, fill, sems = rest[2 * parts :]
    per = each // parts

    def clear_meta(i, _):
        meta[i] = 0
        return 0

    def clear_fill(i, _):
        fill[i] = 0
        return 0

    lax.fori_loop(0, meta.shape[0], clear_meta, 0)
    lax.fori_loop(0, fill.shape[0], clear_fill, 0)

    def send(b, _):
        tile = tiles[b]
        owner = lax.div(tile, local_tiles)
        rank = fill[owner]
        fill[owner] = rank + 1
        slot = owner * each + rank
        meta[2 * slot] = counts[b]
        meta[2 * slot + 1] = tile
        part = lax.div(rank, per)
        place = owner * per + lax.rem(rank, per)
        for c in range(parts):

            @pl.when(part == c)
            def _():
                pltpu.make_async_copy(obs.at[b], obs_out[c].at[place], sems.at[0]).start()
                pltpu.make_async_copy(pix.at[b], pix_out[c].at[place], sems.at[1]).start()

        return 0

    lax.fori_loop(0, obs.shape[0], send, 0)
    pltpu.make_async_copy(obs, obs, sems.at[0]).wait()
    pltpu.make_async_copy(pix, pix, sems.at[1]).wait()


def pack(observations, pixel_geometry, block_counts, block_tiles, devices, local_tiles, parts):
    blocks = observations.shape[0]
    each = 2 * blocks // devices
    per = each // parts
    smem = pl.BlockSpec(memory_space=pltpu.SMEM)
    hbm = pl.BlockSpec(memory_space=pl.ANY)
    out = pl.pallas_call(
        functools.partial(pack_kernel, local_tiles, parts, each),
        in_specs=[smem, smem, hbm, hbm],
        out_specs=[hbm] * (2 * parts) + [smem],
        out_shape=[
            jax.ShapeDtypeStruct((devices * per,) + observations.shape[1:], observations.dtype)
        ]
        * parts
        + [jax.ShapeDtypeStruct((devices * per,) + pixel_geometry.shape[1:], jnp.float32)] * parts
        + [jax.ShapeDtypeStruct((devices * each * 2,), jnp.int32)],
        scratch_shapes=[pltpu.SMEM((devices,), jnp.int32), pltpu.SemaphoreType.DMA((2,))],
        name="pack",
    )(block_tiles, block_counts, observations, pixel_geometry)
    return out[:parts], out[parts : 2 * parts], out[2 * parts]


def fit_kernel(
    first,
    counts,
    tiles,
    cutoffs,
    places,
    obs,
    pix,
    screens,
    stress,
    patches,
    *rest,
):
    if first:
        grad, screen_grad, items, sems = rest
        grad[...] = jnp.zeros_like(grad)
        screen_grad[...] = jnp.zeros_like(screen_grad)
    else:
        grad_in, screen_in, grad, screen_grad, items, sems = rest
        copies = [
            pltpu.make_async_copy(grad_in, grad, sems.at[0]),
            pltpu.make_async_copy(screen_in, screen_grad, sems.at[1]),
        ]
        for copy in copies:
            copy.start()
        for copy in copies:
            copy.wait()
    width = obs.shape[2]
    local_tiles = screens.shape[0]

    def list_slot(s, total):
        live = lax.div(counts[s] + CHUNK - 1, CHUNK)

        def put(c, at):
            items[at] = s * (width // CHUNK) + c
            return at + 1

        return lax.fori_loop(0, live, put, total)

    total = lax.fori_loop(0, obs.shape[0], list_slot, 0)

    def step(i, _):
        item = items[i]
        slot = lax.div(item, width // CHUNK)
        start = pl.multiple_of(lax.rem(item, width // CHUNK) * CHUNK, CHUNK)
        tile = tiles[slot]
        local = lax.rem(tile, local_tiles)
        rows = pix[slot, :, pl.ds(start, CHUNK)]
        columns = rows.T
        east, north = columns[:, 0:1], columns[:, 1:2]
        le, ln, lu = columns[:, 4:5], columns[:, 5:6], columns[:, 6:7]
        greens, nears = [], []
        prediction = jnp.zeros((obs.shape[1], CHUNK), jnp.float32)
        for k in range(NEAR):
            near = cutoffs[tile * NEAR + k]
            patch = patches[near]
            dx = east - patch[0:1]
            dy = north - patch[1:2]
            inverse = lax.rsqrt(dx * dx + dy * dy + patch[3:4])
            along = le * dx + ln * dy + lu * patch[2:3]
            green = (patch[4:5] * along * inverse * inverse * inverse).astype(jnp.bfloat16)
            prediction += lax.dot_general(
                stress[near], green, (((1,), (1,)), ((), ())), preferred_element_type=jnp.float32
            )
            greens.append(green)
            nears.append(near)
        node = lax.broadcasted_iota(jnp.int32, (SG, CHUNK), 0).astype(jnp.float32)
        across = jnp.maximum(0.0, 1.0 - jnp.abs(rows[2:3] - node))
        upward = jnp.maximum(0.0, 1.0 - jnp.abs(rows[3:4] - node))
        hats = jnp.concatenate(
            [(across[a : a + 1] * upward).astype(jnp.bfloat16) for a in range(SG)], axis=0
        )
        correction = jnp.dot(screens[local], hats, preferred_element_type=jnp.float32)
        lane = lax.broadcasted_iota(jnp.int32, (1, CHUNK), 1) + start
        scale = jnp.where(lane < counts[slot], rows[7:8], 0.0)
        observed = obs[slot, :, pl.ds(start, CHUNK)].astype(jnp.float32)
        weighted = ((prediction + correction - observed) * scale).astype(jnp.bfloat16)
        for near, green in zip(nears, greens):
            place = places[near]
            grad[place] += jnp.dot(weighted, green, preferred_element_type=jnp.float32)
        screen_grad[local] += lax.dot_general(
            weighted, hats, (((1,), (1,)), ((), ())), preferred_element_type=jnp.float32
        )
        return 0

    lax.fori_loop(0, total, step, 0)


def fit(counts, tiles, cutoffs, places, obs, pix, screens, stress, patches, state):
    first = state is None
    blocks, epochs = stress.shape[0], stress.shape[1]
    slots, width = obs.shape[0], obs.shape[2]
    vmem = pl.BlockSpec(memory_space=pltpu.VMEM)
    smem = pl.BlockSpec(memory_space=pltpu.SMEM)
    hbm = pl.BlockSpec(memory_space=pl.ANY)
    extra = () if first else tuple(state)
    return pl.pallas_call(
        functools.partial(fit_kernel, first),
        in_specs=[smem] * 4 + [vmem] * 5 + [hbm] * len(extra),
        out_specs=[vmem, vmem],
        out_shape=[
            jax.ShapeDtypeStruct((blocks, epochs, PBLK), jnp.float32),
            jax.ShapeDtypeStruct(screens.shape, jnp.float32),
        ],
        scratch_shapes=[
            pltpu.SMEM((slots * (width // CHUNK),), jnp.int32),
            pltpu.SemaphoreType.DMA((2,)),
        ],
        compiler_params=pltpu.CompilerParams(vmem_limit_bytes=56 * MIB),
        cost_estimate=pl.CostEstimate(
            flops=slots * 4 * epochs * width * (NEAR + 1) * PBLK,
            bytes_accessed=40 * MIB,
            transcendentals=slots * width * NEAR * PBLK,
        ),
        name="fit",
    )(counts, tiles, cutoffs, places, obs, pix, screens, stress, patches, *extra)


def reduce_scatter(grad, devices):
    stages = devices.bit_length() - 1
    for bit in range(stages):
        half = grad.shape[0] // 2
        kept, given = grad[:half], grad[half:]
        if stages - bit <= NARROW:
            given = given.astype(jnp.bfloat16)
        pairs = [(i, i ^ (1 << bit)) for i in range(devices)]
        grad = kept + lax.ppermute(given, "tile", pairs).astype(jnp.float32)
    return grad


def on_device(
    observations,
    pixel_geometry,
    block_counts,
    block_tiles,
    cutoff_lists,
    patch_geometry,
    stress,
    screens,
):
    devices = lax.axis_size("tile")
    here = lax.axis_index("tile")
    local_tiles = screens.shape[0]
    blocks, epochs, width = observations.shape
    each = 2 * blocks // devices
    parts = min(PARTS, each)
    per = each // parts
    local = stress.shape[1] // PBLK
    mine = jnp.swapaxes(stress.reshape(epochs, local, PBLK), 0, 1)
    full = lax.all_gather(mine, "tile", axis=0, tiled=True)
    patch_blocks = full.shape[0]
    east, north, depth, compliance = patch_geometry
    patches = jnp.stack(
        [east, north, depth, depth * depth, compliance * depth * depth] + [depth] * 3
    )
    patches = jnp.swapaxes(patches.reshape(8, patch_blocks, PBLK), 0, 1)
    stages = devices.bit_length() - 1
    block = jnp.arange(patch_blocks)
    other = (block // local) ^ here
    turned = sum(((other >> b) & 1) << (stages - 1 - b) for b in range(stages))
    places = (turned * local + block % local).astype(jnp.int32)

    obs_parts, pix_parts, meta = pack(
        observations, pixel_geometry, block_counts, block_tiles, devices, local_tiles, parts
    )

    def swap(values):
        split = values.reshape((devices, -1) + values.shape[1:])
        got = lax.all_to_all(split, "tile", split_axis=0, concat_axis=0, tiled=True)
        return got.reshape(values.shape)

    info = swap(meta).reshape(devices, each, 2)
    cutoffs = cutoff_lists.reshape(-1)
    state = None
    for part, (obs, pix) in enumerate(zip(obs_parts, pix_parts)):
        here_info = info[:, part * per : (part + 1) * per].reshape(devices * per, 2)
        state = fit(
            here_info[:, 0],
            here_info[:, 1],
            cutoffs,
            places,
            swap(obs),
            swap(pix),
            screens,
            full,
            patches,
            state,
        )
    grad, screen_gradient = state
    grad = reduce_scatter(grad, devices)
    return (jnp.swapaxes(grad, 0, 1).reshape(epochs, local * PBLK), screen_gradient)


def solution(mesh):
    return jax.shard_map(
        on_device,
        mesh=mesh,
        in_specs=(
            P(("groups", "tile"), None, None),
            P(("groups", "tile"), None, None),
            P(("groups", "tile")),
            P(("groups", "tile")),
            P(),
            P(),
            P(None, ("groups", "tile")),
            P(("groups", "tile"), None, None),
        ),
        out_specs=(P(None, ("groups", "tile")), P(("groups", "tile"), None, None)),
        check_vma=False,
    )
```

time: 857 us -> 463 us (0.54)
  local copies, waits for them, and re-layouts: 222 us -> 11.4 us
  matrix products: 201 us -> 0 us
  Pallas kernels: 0 us -> 192 us
  other arithmetic: 160 us -> 2.48 us
  waiting for transfers between devices: 226 us -> 104 us
  starting transfers between devices: 23.8 us -> 86.4 us
  blocking collectives: 0 us -> 51 us
    dot_general x64 -> x0, matrix products: 201 us -> none  [the longest x16 87.7 us: one(): jnp.dot(weighted, green, preferred_element_type=jnp.float32)]
    pallas_call x0 -> x3, Pallas kernels: none -> 192 us  [the longest x2 109 us: fit(): pl.pallas_call(functools.partial(fit_kernel, first), in_specs=[smem] * 4...]
    scatter-add x32 -> x0, other arithmetic: 148 us -> none  [the longest x16 104 us: add_terms(): return grad.at[:, near.reshape(-1)].add(flat)]
    reduce_scatter x1 -> x0, waiting for transfers between devices: 121 us -> none  [on_device(): lax.psum_scatter(grad.reshape((epochs, patch_count)), 'tile', scatter_dim...]
    gather x96 -> x0, local copies, waits for them, and re-layouts: 111 us -> none  [the longest x16 44.6 us: near_pieces(): stress_near = stress_blocks[:, near].reshape(stress_blocks.shape[0], -1)]
    ppermute x0 -> x4, starting transfers between devices: none -> 56.9 us  [reduce_scatter(): grad = kept + lax.ppermute(given, 'tile', pairs).astype(jnp.float32)]
    ppermute x0 -> x4, waiting for transfers between devices: none -> 55.1 us  [reduce_scatter(): grad = kept + lax.ppermute(given, 'tile', pairs).astype(jnp.float32)]
    reshape x51 -> x4, local copies, waits for them, and re-layouts: 56.6 us -> 1.82 us  [the longest x1 0.84 us: on_device(): jnp.swapaxes(grad, 0, 1).reshape(epochs, local * PBLK)]
  transfers between devices with their start and end apart: 5 -> 7, of which waited for: 4 -> 5; matrix products, arithmetic and copies ran while one was open for 3% -> 1% of each run, Pallas kernels for 0% -> 15%
where the time goes in v1:
time: 463 us; the launch traced here: 461 us
  Pallas kernels  192 us (41%)
  waiting for transfers between devices  104 us (22%)
  starting transfers between devices  86.4 us (19%)
  blocking collectives  51 us (11%)
  between operations  14.2 us (3%)
  local copies, waits for them, and re-layouts  11.4 us (2%)
    pallas_call x2, Pallas kernels, fit(): pl.pallas_call(functools.partial(fit_kernel, first), in_specs=[smem] * 4...  109 us
    pallas_call x1, Pallas kernels, pack(): pl.pallas_call(functools.partial(pack_kernel, local_tiles, parts, each),...  83.5 us
    ppermute x4, starting transfers between devices, reduce_scatter(): grad = kept + lax.ppermute(given, 'tile', pairs).astype(jnp.float32)  56.9 us
    ppermute x4, waiting for transfers between devices, reduce_scatter(): grad = kept + lax.ppermute(given, 'tile', pairs).astype(jnp.float32)  55.1 us
    all_to_all x3, blocking collectives, swap(): got = lax.all_to_all(split, 'tile', split_axis=0, concat_axis=0, tiled=True)  51 us
    all_to_all x2, waiting for transfers between devices, swap(): got = lax.all_to_all(split, 'tile', split_axis=0, concat_axis=0, tiled=True)  48.6 us
    all_to_all x2, starting transfers between devices, swap(): got = lax.all_to_all(split, 'tile', split_axis=0, concat_axis=0, tiled=True)  29.5 us
  transfers between devices with their start and end apart: 7, of which 5 were waited for; matrix products, arithmetic and copies ran while one was open for 1% of the time, Pallas kernels for 15%

profile of v1, /device:TPU:0, one launch (start us, length us, event | category | flops | bytes accessed | tf_op | source)
XLA Modules:
  0.0 461.4 jit_solution(13436847109422406899)
XLA Ops:
  7.2 83.5 %pack.1 = (bf16[64,64,256]{2,1,0:T(8,128)(2,1)}, bf16[64,64,256]{2,1,0:T(8,128)(2,1)}, f32[64,8,256]{2,1,0:T(8,128)}, f32[64,8,256]{2,1,0:T(8,128)}, s32[256]{0:T(256)}) custom-call(s32[64]{0:T(128)} %tiles.1, s32[64]{0:T(128)} %counts.1, bf16[64,64,256]{2,1,0:T(8,128)(2,1)} %obs.1, f32[64,8,256]{2,1,0:T(8,128)} %pix.1), custom_call_target="tpu_custom_call" | custom-call | tf_op jit(solution)/shard_map/pack/pallas_call | solution.py:65
  90.7 0.7 all_to_all.18
  91.4 13.6 %all_to_all.29 = s32[16,1,16]{2,1,0:T(1,128)S(1)} all-to-all(s32[16,1,16]{2,1,0:T(1,128)S(1)} %bitcast.54), channel_id=1, replica_groups=mesh['groups'=2,'tile'=16] {'tile'}, dimensions={0} | all-to-all | bytes 2048 | tf_op jit(solution)/shard_map/all_to_all | solution.py:249
  105.0 18.7 %all_to_all.30 = f32[16,4,8,256]{3,2,1,0:T(8,128)} all-to-all(f32[16,4,8,256]{3,2,1,0:T(8,128)} %bitcast.51), channel_id=1, replica_groups=mesh['groups'=2,'tile'=16] {'tile'}, dimensions={0} | all-to-all | bytes 1048576 | tf_op jit(solution)/shard_map/all_to_all | solution.py:249
  123.7 18.7 %all_to_all.31 = f32[16,4,8,256]{3,2,1,0:T(8,128)} all-to-all(f32[16,4,8,256]{3,2,1,0:T(8,128)} %bitcast.50), channel_id=1, replica_groups=mesh['groups'=2,'tile'=16] {'tile'}, dimensions={0} | all-to-all | bytes 1048576 | tf_op jit(solution)/shard_map/all_to_all | solution.py:249
  142.4 4.1 all-to-all-start.3
  146.7 0.8 copy.25
  147.5 48.6 %all-to-all-done.3 = bf16[16,4,64,256]{3,2,1,0:T(8,128)(2,1)S(1)} async-done(((bf16[16,4,64,256]{3,2,1,0:T(8,128)(2,1)}), bf16[16,4,64,256]{3,2,1,0:T(8,128)(2,1)S(1)}, u32[]{:S(2)}, u32[]{:S(2)}) %all-to-all-start.3) | async-done | bytes 2097184 | tf_op jit(solution)/shard_map/all_to_all | solution.py:249
  196.1 1.3 copy-done.1
  197.4 25.3 %all-to-all-start.1 = ((bf16[16,4,64,256]{3,2,1,0:T(8,128)(2,1)}), bf16[16,4,64,256]{3,2,1,0:T(8,128)(2,1)}, u32[]{:S(2)}, u32[]{:S(2)}) async-start(bf16[16,4,64,256]{3,2,1,0:T(8,128)(2,1)} %bitcast.4), calls=%async_computation.1 | async-start | bytes 4194304 | tf_op jit(solution)/shard_map/all_to_all | solution.py:249
  223.2 0.8 reshape.56.cutoffs
  224.0 2.3 stack.18
  227.9 0.6 slice_bitcast_fusion.2
  228.5 71.3 %fit.2 = (f32[128,64,256]{2,1,0:T(8,128)}, f32[32,64,256]{2,1,0:T(8,128)}) custom-call(s32[64]{0:T(128)} %get-tuple-element.26.counts, s32[64]{0:T(128)} %get-tuple-element.25.tiles, s32[1536]{0:T(1024)} %reshape.56.cutoffs, s32[128]{0:T(128)} %fusion.1.places, bf16[64,64,256]{2,1,0:T(8,128)(2,1)} %bitcast.39, f32[64,8,256]{2,1,0:T(8,128)} %bitcast.48, ...), custom_call_target="tpu_custom_call" | custom-call | flops 4294967296 | bytes 41943040 | tf_op jit(solution)/shard_map/fit/pallas_call | solution.py:177
  299.8 37.3 %fit.3 = (f32[128,64,256]{2,1,0:T(8,128)}, f32[32,64,256]{2,1,0:T(8,128)}) custom-call(s32[64]{0:T(128)} %get-tuple-element.28.counts, s32[64]{0:T(128)} %get-tuple-element.27.tiles, s32[1536]{0:T(1024)} %reshape.56.cutoffs, s32[128]{0:T(128)} %fusion.1.places, bf16[64,64,256]{2,1,0:T(8,128)(2,1)} %bitcast.5.obs, f32[64,8,256]{2,1,0:T(8,128)} %bitcast.47, ...), custom_call_target="tpu_custom_call" | custom-call | flops 4294967296 | bytes 41943040 | tf_op jit(solution)/shard_map/fit/pallas_call | solution.py:177
  337.0 2.6 slice.53
  339.8 7.1 %collective-permute-done = f32[64,64,256]{2,1,0:T(8,128)S(1)} collective-permute-done((f32[64,64,256]{2,1,0:T(8,128)S(1)}, f32[64,64,256]{2,1,0:T(8,128)S(1)}, u32[]{:S(2)}, u32[]{:S(2)}) %collective-permute-start) | collective-permute-done | bytes 4194336 | tf_op jit(solution)/shard_map/ppermute | solution.py:207
  346.9 1.1 slice_add_fusion
  348.2 25.2 %collective-permute-done.1 = bf16[32,64,256]{2,1,0:T(8,128)(2,1)S(1)} collective-permute-done((bf16[32,64,256]{2,1,0:T(8,128)(2,1)S(1)}, bf16[32,64,256]{2,1,0:T(8,128)(2,1)S(1)}, u32[]{:S(2)}, u32[]{:S(2)}) %collective-permute-start.1) | collective-permute-done | bytes 1048608 | tf_op jit(solution)/shard_map/ppermute | solution.py:207
  373.9 53.8 %collective-permute-start.2 = (bf16[16,64,256]{2,1,0:T(8,128)(2,1)S(1)}, bf16[16,64,256]{2,1,0:T(8,128)(2,1)S(1)}, u32[]{:S(2)}, u32[]{:S(2)}) collective-permute-start(bf16[16,64,256]{2,1,0:T(8,128)(2,1)S(1)} %slice.82), channel_id=1, source_target_pairs={{0,4},{1,5},{2,6},{3,7},{4,0},{5,1},{6,2},{7,3},{8,12},{9,13},{10,... | collective-permute-start | bytes 1572872 | tf_op jit(solution)/shard_map/ppermute | solution.py:207
  427.7 11.6 %collective-permute-done.2 = bf16[16,64,256]{2,1,0:T(8,128)(2,1)S(1)} collective-permute-done((bf16[16,64,256]{2,1,0:T(8,128)(2,1)S(1)}, bf16[16,64,256]{2,1,0:T(8,128)(2,1)S(1)}, u32[]{:S(2)}, u32[]{:S(2)}) %collective-permute-start.2) | collective-permute-done | bytes 524320 | tf_op jit(solution)/shard_map/ppermute | solution.py:207
  439.5 3.0 collective-permute-start.3
  442.5 11.1 %collective-permute-done.3 = bf16[8,64,256]{2,1,0:T(8,128)(2,1)S(1)} collective-permute-done((bf16[8,64,256]{2,1,0:T(8,128)(2,1)S(1)}, bf16[8,64,256]{2,1,0:T(8,128)(2,1)S(1)}, u32[]{:S(2)}, u32[]{:S(2)}) %collective-permute-start.3) | collective-permute-done | bytes 262176 | tf_op jit(solution)/shard_map/ppermute | solution.py:207
  453.7 0.8 copy.28
  (32 shorter events, 3.1 us)
Async XLA Ops:
  142.4 4.2 copy-start.3
  142.4 53.7 %all-to-all-start.3 = ((bf16[16,4,64,256]{3,2,1,0:T(8,128)(2,1)}), bf16[16,4,64,256]{3,2,1,0:T(8,128)(2,1)S(1)}, u32[]{:S(2)}, u32[]{:S(2)}) async-start(bf16[16,4,64,256]{3,2,1,0:T(8,128)(2,1)} %bitcast.40), calls=%async_computation.3 | async-start | bytes 4194304 | tf_op jit(solution)/shard_map/all_to_all | solution.py:249
  146.6 81.9 %all-gather.2.cloned.1.call-start = ((), (), s32[]{:S(2)}) async-start(), calls=%async_computation.5 | async-start | bytes 4456448 | tf_op jit(solution)/shard_map/all_gather | solution.py:230
  196.1 1.3 copy-start.1
  196.1 26.7 %copy-start.2 = (f32[4,32768]{1,0:T(4,128)S(1)}, f32[4,32768]{1,0:T(4,128)}, u32[]{:S(2)}) copy-start(f32[4,32768]{1,0:T(4,128)} %param.13) | copy-start | bytes 1572868
  196.1 27.0 %copy-start.4 = (s32[512,3]{0,1:T(4,128)S(1)}, s32[512,3]{0,1:T(4,128)}, u32[]{:S(2)}) copy-start(s32[512,3]{0,1:T(4,128)} %param.12) | copy-start | bytes 18436
  197.4 102.3 %all-to-all-start.1 = ((bf16[16,4,64,256]{3,2,1,0:T(8,128)(2,1)}), bf16[16,4,64,256]{3,2,1,0:T(8,128)(2,1)}, u32[]{:S(2)}, u32[]{:S(2)}) async-start(bf16[16,4,64,256]{3,2,1,0:T(8,128)(2,1)} %bitcast.4), calls=%async_computation.1 | async-start | bytes 4194304 | tf_op jit(solution)/shard_map/all_to_all | solution.py:249
  337.0 9.9 %copy-start = (f32[128,64,256]{2,1,0:T(8,128)S(1)}, f32[128,64,256]{2,1,0:T(8,128)}, u32[]{:S(2)}) copy-start(f32[128,64,256]{2,1,0:T(8,128)} %get-tuple-element.18) | copy-start | bytes 25165828
  339.7 7.2 %collective-permute-start = (f32[64,64,256]{2,1,0:T(8,128)S(1)}, f32[64,64,256]{2,1,0:T(8,128)S(1)}, u32[]{:S(2)}, u32[]{:S(2)}) collective-permute-start(f32[64,64,256]{2,1,0:T(8,128)S(1)} %slice.53), channel_id=1, source_target_pairs={{0,1},{1,0},{2,3},{3,2},{4,5},{5,4},{6,7},{7,6},{8,9},{9,8},{10,11... | collective-permute-start | bytes 12582920 | tf_op jit(solution)/shard_map/ppermute | solution.py:207
  348.1 25.3 %collective-permute-start.1 = (bf16[32,64,256]{2,1,0:T(8,128)(2,1)S(1)}, bf16[32,64,256]{2,1,0:T(8,128)(2,1)S(1)}, u32[]{:S(2)}, u32[]{:S(2)}) collective-permute-start(bf16[32,64,256]{2,1,0:T(8,128)(2,1)S(1)} %slice.81), channel_id=1, source_target_pairs={{0,2},{1,3},{2,0},{3,1},{4,6},{5,7},{6,4},{7,5},{8,10},{9,11},{10,... | collective-permute-start | bytes 3145736 | tf_op jit(solution)/shard_map/ppermute | solution.py:207
  373.9 65.5 %collective-permute-start.2 = (bf16[16,64,256]{2,1,0:T(8,128)(2,1)S(1)}, bf16[16,64,256]{2,1,0:T(8,128)(2,1)S(1)}, u32[]{:S(2)}, u32[]{:S(2)}) collective-permute-start(bf16[16,64,256]{2,1,0:T(8,128)(2,1)S(1)} %slice.82), channel_id=1, source_target_pairs={{0,4},{1,5},{2,6},{3,7},{4,0},{5,1},{6,2},{7,3},{8,12},{9,13},{10,... | collective-permute-start | bytes 1572872 | tf_op jit(solution)/shard_map/ppermute | solution.py:207
  439.5 14.1 %collective-permute-start.3 = (bf16[8,64,256]{2,1,0:T(8,128)(2,1)S(1)}, bf16[8,64,256]{2,1,0:T(8,128)(2,1)S(1)}, u32[]{:S(2)}, u32[]{:S(2)}) collective-permute-start(bf16[8,64,256]{2,1,0:T(8,128)(2,1)S(1)} %slice.83), channel_id=1, source_target_pairs={{0,8},{1,9},{2,10},{3,11},{4,12},{5,13},{6,14},{7,15},{8,0},{9,1},... | collective-permute-start | bytes 786440 | tf_op jit(solution)/shard_map/ppermute | solution.py:207
Sparse Core Ops, SparseCore 0:
  150.1 72.4 all-gather.1

commit v2 on v0

v2 whole, which is shorter than its diff:
```python
import functools

import jax
import jax.numpy as jnp
from jax import lax
from jax.experimental import pallas as pl
from jax.experimental.pallas import tpu as pltpu
from jax.sharding import PartitionSpec as P

PBLK = 256
NEAR = 3
SG = 16
CHUNK = 128
LAYER = 4
PAIR = 2
NARROW = 3
MIB = 1 << 20


def pack_kernel(local_tiles, layers, each, here, tiles, counts, obs, pix, *rest):
    obs_out, pix_out = rest[: 2 * layers], rest[2 * layers : 3 * layers]
    obs_all, pix_all, fill, sems = rest[3 * layers :]
    my_layer, my_seat = lax.div(here[0], LAYER), lax.rem(here[0], LAYER)
    width = pix.shape[2]

    def clear(i, _):
        fill[i] = 0
        return 0

    lax.fori_loop(0, fill.shape[0], clear, 0)
    for x in range(layers):
        pix_all[x, LAYER * each] = jnp.zeros((8, width), jnp.float32)
    lane = lax.broadcasted_iota(jnp.int32, (8, width), 1)
    row = lax.broadcasted_iota(jnp.int32, (8, width), 0)

    def put(b, _):
        tile = tiles[b]
        owner = lax.div(tile, local_tiles)
        rank = fill[owner]
        fill[owner] = rank + 1
        x = lax.div(owner, LAYER) ^ my_layer
        seat = lax.rem(owner, LAYER) ^ my_seat
        half = 1 - lax.div(seat, PAIR)
        place = ((half * layers + x) * PAIR + lax.rem(seat, PAIR)) * each + rank
        slot = seat * each + rank
        obs_all[place] = obs[b]
        pix_all[x, slot] = pix[b]
        entry = jnp.where(row == 0, counts[b], tile).astype(jnp.float32)
        info = pix_all[x, LAYER * each]
        pix_all[x, LAYER * each] = jnp.where((lane == slot) & (row < 2), entry, info)
        return 0

    lax.fori_loop(0, obs.shape[0], put, 0)
    span = PAIR * each
    copies = [
        pltpu.make_async_copy(pix_all.at[x], pix_out[x], sems.at[x]) for x in range(layers)
    ] + [
        pltpu.make_async_copy(obs_all.at[pl.ds(i * span, span)], obs_out[i], sems.at[layers + i])
        for i in range(2 * layers)
    ]
    for copy in copies:
        copy.start()
    for copy in copies:
        copy.wait()


def pack(observations, pixel_geometry, block_counts, block_tiles, here, devices, local_tiles):
    blocks, epochs, width = observations.shape
    each = 2 * blocks // devices
    layers = devices // LAYER
    smem = pl.BlockSpec(memory_space=pltpu.SMEM)
    vmem = pl.BlockSpec(memory_space=pltpu.VMEM)
    hbm = pl.BlockSpec(memory_space=pl.ANY)
    obs_part = jax.ShapeDtypeStruct((PAIR * each, epochs, width), observations.dtype)
    pix_part = jax.ShapeDtypeStruct((LAYER * each + 1, 8, width), jnp.float32)
    out = pl.pallas_call(
        functools.partial(pack_kernel, local_tiles, layers, each),
        in_specs=[smem, smem, smem, vmem, vmem],
        out_specs=[hbm] * (3 * layers),
        out_shape=[obs_part] * (2 * layers) + [pix_part] * layers,
        scratch_shapes=[
            pltpu.VMEM((devices * each, epochs, width), observations.dtype),
            pltpu.VMEM((layers,) + pix_part.shape, jnp.float32),
            pltpu.SMEM((devices,), jnp.int32),
            pltpu.SemaphoreType.DMA((3 * layers,)),
        ],
        compiler_params=pltpu.CompilerParams(vmem_limit_bytes=24 * MIB),
        name="pack",
    )(here, block_tiles, block_counts, observations, pixel_geometry)
    return out[:layers], out[layers : 2 * layers], out[2 * layers :]


def fit_kernel(first, layers, each, *refs):
    info, cutoffs, places = refs[:3]
    obs_in, pix_in = refs[3 : 3 + layers], refs[3 + layers : 3 + 2 * layers]
    rest = refs[3 + 2 * layers :]
    screen_in, stress_in, patches_in = rest[:2], rest[2], rest[3]
    if first:
        grad_out, screen_out = rest[4:5], rest[5:7]
        rest = rest[7:]
    else:
        grad_in, grad_out, screen_out = rest[4], rest[5:7], rest[7:9]
        rest = rest[9:]
    obs, pix, screens, stress, patches, grad, screen_grad = rest[:7]
    green_a, hats_a, green_b, hats_b, items, sems = rest[7:]
    span = PAIR * each
    base = span if first else 0
    local_tiles = screens.shape[0] // 2
    width = obs.shape[2]
    chunks = width // CHUNK

    loads = [
        (stress_in, stress),
        (patches_in, patches),
        (screen_in[0], screens.at[pl.ds(0, local_tiles)]),
        (screen_in[1], screens.at[pl.ds(local_tiles, local_tiles)]),
    ]
    for x in range(layers):
        loads.append((pix_in[x].at[pl.ds(base, span)], pix.at[pl.ds(x * span, span)]))
        loads.append((obs_in[x], obs.at[pl.ds(x * span, span)]))
    if not first:
        loads.append((grad_in, grad))
    loads = [pltpu.make_async_copy(a, b, sems.at[i]) for i, (a, b) in enumerate(loads)]
    for copy in loads:
        copy.start()
    screen_grad[...] = jnp.zeros_like(screen_grad)
    if first:
        grad[...] = jnp.zeros_like(grad)

    def count_of(slot):
        return info[lax.div(slot, span) * 2 * LAYER * each + base + lax.rem(slot, span)]

    def tile_of(slot):
        return info[(lax.div(slot, span) * 2 + 1) * LAYER * each + base + lax.rem(slot, span)]

    def list_slot(slot, total):
        live = lax.div(count_of(slot) + CHUNK - 1, CHUNK)

        def put(c, at):
            items[at] = slot * chunks + c
            return at + 1

        return lax.fori_loop(0, live, put, total)

    total = lax.fori_loop(0, layers * span, list_slot, 0)
    for copy in loads:
        copy.wait()

    def item_of(i):
        item = items[jnp.minimum(i, total - 1)]
        slot = lax.div(item, chunks)
        start = pl.multiple_of(lax.rem(item, chunks) * CHUNK, CHUNK)
        return slot, start, tile_of(slot)

    def make(i, green, hats):
        slot, start, tile = item_of(i)
        rows = pix[slot, :, pl.ds(start, CHUNK)]
        columns = rows.T
        near = [cutoffs[tile * NEAR + k] for k in range(NEAR)]
        for low in range(0, CHUNK, 16):
            strips = [[] for _ in range(NEAR)]
            for at in (low, low + 8):
                east, north, le, ln, lu = (
                    jnp.broadcast_to(columns[at : at + 8, c : c + 1], (8, PBLK))
                    for c in (0, 1, 4, 5, 6)
                )
                for k in range(NEAR):
                    patch = patches.at[near[k]]
                    dx = east - patch[0]
                    dy = north - patch[1]
                    inverse = lax.rsqrt(dx * dx + dy * dy + patch[3])
                    along = le * dx + ln * dy + lu * patch[2]
                    strips[k].append(patch[4] * along * inverse * inverse * inverse)
            for k in range(NEAR):
                green[low : low + 16, k * PBLK : (k + 1) * PBLK] = jnp.concatenate(
                    strips[k], axis=0
                ).astype(jnp.bfloat16)
        node = lax.broadcasted_iota(jnp.int32, (SG, CHUNK), 0).astype(jnp.float32)
        across = jnp.maximum(0.0, 1.0 - jnp.abs(rows[2:3] - node))
        upward = jnp.maximum(0.0, 1.0 - jnp.abs(rows[3:4] - node))
        for a in range(SG):
            hats[a * SG : (a + 1) * SG] = (across[a : a + 1] * upward).astype(jnp.bfloat16)

    def use(i, green, hats):
        slot, start, tile = item_of(i)
        near = [cutoffs[tile * NEAR + k] for k in range(NEAR)]
        screen = lax.div(lax.rem(slot, span), each) * local_tiles + lax.rem(tile, local_tiles)
        model = jnp.dot(screens[screen], hats[...], preferred_element_type=jnp.float32)
        for k in range(NEAR):
            model += lax.dot_general(
                stress[near[k]],
                green[:, k * PBLK : (k + 1) * PBLK],
                (((1,), (1,)), ((), ())),
                preferred_element_type=jnp.float32,
            )
        live = jnp.where(i < total, count_of(slot), 0) - start
        lane = lax.broadcasted_iota(jnp.int32, (1, CHUNK), 1)
        scale = jnp.where(lane < live, pix[slot, 7:8, pl.ds(start, CHUNK)], 0.0)
        observed = obs[slot, :, pl.ds(start, CHUNK)].astype(jnp.float32)
        weighted = ((model - observed) * scale).astype(jnp.bfloat16)
        for k in range(NEAR):
            grad[places[near[k]]] += jnp.dot(
                weighted,
                green[:, k * PBLK : (k + 1) * PBLK],
                preferred_element_type=jnp.float32,
            )
        screen_grad[screen] += lax.dot_general(
            weighted, hats[...], (((1,), (1,)), ((), ())), preferred_element_type=jnp.float32
        )

    @pl.when(total > 0)
    def _():
        make(0, green_a, hats_a)

        def step(j, _):
            use(2 * j, green_a, hats_a)
            make(2 * j + 1, green_b, hats_b)
            use(2 * j + 1, green_b, hats_b)
            make(2 * j + 2, green_a, hats_a)
            return 0

        lax.fori_loop(0, lax.div(total + 1, 2), step, 0)

    part = grad.shape[0] // len(grad_out)
    stores = [(grad.at[pl.ds(i * part, part)], out) for i, out in enumerate(grad_out)] + [
        (screen_grad.at[pl.ds(i * local_tiles, local_tiles)], out)
        for i, out in enumerate(screen_out)
    ]
    stores = [pltpu.make_async_copy(a, b, sems.at[i]) for i, (a, b) in enumerate(stores)]
    for copy in stores:
        copy.start()
    for copy in stores:
        copy.wait()


def fit(info, cutoffs, places, obs, pix, screens, stress, patches, grad):
    first = grad is None
    layers = len(obs)
    blocks, epochs = stress.shape[0], stress.shape[1]
    span, width = obs[0].shape[0], obs[0].shape[2]
    slots = layers * span
    local_tiles = screens[0].shape[0]
    smem = pl.BlockSpec(memory_space=pltpu.SMEM)
    hbm = pl.BlockSpec(memory_space=pl.ANY)
    extra = () if first else (grad,)
    pieces = 1 if first else 2
    grad_part = jax.ShapeDtypeStruct((blocks // pieces, epochs, PBLK), jnp.float32)
    screen_part = jax.ShapeDtypeStruct(screens[0].shape, jnp.float32)
    out = pl.pallas_call(
        functools.partial(fit_kernel, first, layers, span // PAIR),
        in_specs=[smem] * 3 + [hbm] * (2 * layers + 4 + len(extra)),
        out_specs=[hbm] * (pieces + 2),
        out_shape=[grad_part] * pieces + [screen_part] * 2,
        scratch_shapes=[
            pltpu.VMEM((slots, epochs, width), obs[0].dtype),
            pltpu.VMEM((slots, 8, width), jnp.float32),
            pltpu.VMEM((2 * local_tiles,) + screens[0].shape[1:], screens[0].dtype),
            pltpu.VMEM(stress.shape, stress.dtype),
            pltpu.VMEM(patches.shape, patches.dtype),
            pltpu.VMEM((blocks, epochs, PBLK), jnp.float32),
            pltpu.VMEM((2 * local_tiles,) + screens[0].shape[1:], jnp.float32),
        ]
        + [
            pltpu.VMEM((CHUNK, NEAR * PBLK), jnp.bfloat16),
            pltpu.VMEM((SG * SG, CHUNK), jnp.bfloat16),
        ]
        * 2
        + [
            pltpu.SMEM((slots * (width // CHUNK),), jnp.int32),
            pltpu.SemaphoreType.DMA((5 + 2 * layers,)),
        ],
        compiler_params=pltpu.CompilerParams(vmem_limit_bytes=40 * MIB),
        cost_estimate=pl.CostEstimate(
            flops=slots * 4 * epochs * width * (NEAR + 1) * PBLK,
            bytes_accessed=40 * MIB,
            transcendentals=slots * width * NEAR * PBLK,
        ),
        name="fit",
    )(info, cutoffs, places, *obs, *pix, *screens, stress, patches, *extra)
    return out[:pieces], out[pieces:]


def partner(values, devices, distance):
    return lax.ppermute(values, "tile", [(i, i ^ distance) for i in range(devices)])


def orders(devices):
    stages = devices.bit_length() - 1
    high = list(range(stages - 1, 1, -1))
    return [1] + high, high + [1]


def block_places(devices, here, blocks, local):
    block = jnp.arange(blocks)
    other = (block // local) ^ here
    seat = block % local
    half = local // 2
    spots = []
    for order in orders(devices):
        spot = 0
        for bit in order:
            spot = spot * 2 + ((other >> bit) & 1)
        spots.append(spot)
    chips = devices // 2
    upper = seat // half
    spot = jnp.where(upper == 0, spots[0], spots[1])
    place = (((other & 1) * 2 + upper) * chips + spot) * half + seat % half
    return place.astype(jnp.int32)


def halve(kept, given, devices):
    total = kept + partner(given, devices, 1)
    middle = total.shape[0] // 2
    parts = [total[:middle], total[middle:]]
    both = orders(devices)
    stages = len(both[0])
    for stage in range(stages):
        for side in range(2):
            size = parts[side].shape[0] // 2
            given = parts[side][size:]
            if stages - stage <= NARROW:
                given = given.astype(jnp.bfloat16)
            got = partner(given, devices, 1 << both[side][stage])
            parts[side] = parts[side][:size] + got.astype(jnp.float32)
    return jnp.concatenate(parts, axis=0)


def on_device(
    observations,
    pixel_geometry,
    block_counts,
    block_tiles,
    cutoff_lists,
    patch_geometry,
    stress,
    screens,
):
    devices = lax.axis_size("tile")
    here = lax.axis_index("tile")
    blocks, epochs, width = observations.shape
    local_tiles = screens.shape[0]
    layers = devices // LAYER
    local = stress.shape[1] // PBLK
    each = 2 * blocks // devices

    across = partner(screens, devices, PAIR)
    obs, obs_near, pix = pack(
        observations,
        pixel_geometry,
        block_counts,
        block_tiles,
        jnp.reshape(here, (1,)).astype(jnp.int32),
        devices,
        local_tiles,
    )
    pix = [pix[0]] + [partner(pix[x], devices, x * LAYER) for x in range(1, layers)]
    obs = [obs[0]] + [partner(obs[x], devices, x * LAYER) for x in range(1, layers)]
    obs_near = [obs_near[0]] + [partner(obs_near[x], devices, x * LAYER) for x in range(1, layers)]
    beside, corner = partner(screens, devices, 1), partner(across, devices, 1)

    mine = jnp.swapaxes(stress.reshape(epochs, local, PBLK), 0, 1)
    full = lax.all_gather(mine, "tile", axis=0, tiled=True)
    patch_blocks = full.shape[0]
    east, north, depth, compliance = patch_geometry
    patches = jnp.stack([east, north, depth, depth * depth, compliance * depth * depth])
    patches = jnp.swapaxes(patches.reshape(5, patch_blocks, PBLK), 0, 1)
    patches = jnp.broadcast_to(patches[:, :, None, :], (patch_blocks, 5, 8, PBLK))
    places = block_places(devices, here, patch_blocks, local)
    cutoffs = cutoff_lists.reshape(-1)
    slots = LAYER * each
    info = jnp.stack([p[slots, :2, :slots] for p in pix]).astype(jnp.int32).reshape(-1)

    grad, (far, diagonal) = fit(
        info, cutoffs, places, obs, pix, (across, corner), full, patches, None
    )
    there = (far + partner(diagonal, devices, 1)).astype(jnp.bfloat16)
    back = partner(there, devices, PAIR)
    (kept, given), (own, next_door) = fit(
        info, cutoffs, places, obs_near, pix, (screens, beside), full, patches, grad[0]
    )
    screen_gradient = own + partner(next_door, devices, 1) + back.astype(jnp.float32)
    grad = halve(kept, given, devices)
    return (jnp.swapaxes(grad, 0, 1).reshape(epochs, local * PBLK), screen_gradient)


def solution(mesh):
    return jax.shard_map(
        on_device,
        mesh=mesh,
        in_specs=(
            P(("groups", "tile"), None, None),
            P(("groups", "tile"), None, None),
            P(("groups", "tile")),
            P(("groups", "tile")),
            P(),
            P(),
            P(None, ("groups", "tile")),
            P(("groups", "tile"), None, None),
        ),
        out_specs=(P(None, ("groups", "tile")), P(("groups", "tile"), None, None)),
        check_vma=False,
    )
```

time: 857 us -> 323 us (0.38)
  local copies, waits for them, and re-layouts: 222 us -> 19.6 us
  matrix products: 201 us -> 0 us
  other arithmetic: 160 us -> 5.85 us
  waiting for transfers between devices: 226 us -> 145 us
  Pallas kernels: 0 us -> 61.5 us
  starting transfers between devices: 23.8 us -> 70.7 us
    dot_general x64 -> x0, matrix products: 201 us -> none  [the longest x16 87.7 us: one(): jnp.dot(weighted, green, preferred_element_type=jnp.float32)]
    scatter-add x32 -> x0, other arithmetic: 148 us -> none  [the longest x16 104 us: add_terms(): return grad.at[:, near.reshape(-1)].add(flat)]
    ppermute x0 -> x22, waiting for transfers between devices: none -> 145 us  [partner(): lax.ppermute(values, 'tile', [(i, i ^ distance) for i in range(devices)])]
    reduce_scatter x1 -> x0, waiting for transfers between devices: 121 us -> none  [on_device(): lax.psum_scatter(grad.reshape((epochs, patch_count)), 'tile', scatter_dim...]
    gather x96 -> x0, local copies, waits for them, and re-layouts: 111 us -> none  [the longest x16 44.6 us: near_pieces(): stress_near = stress_blocks[:, near].reshape(stress_blocks.shape[0], -1)]
    ppermute x0 -> x22, starting transfers between devices: none -> 70.7 us  [partner(): lax.ppermute(values, 'tile', [(i, i ^ distance) for i in range(devices)])]
    pallas_call x0 -> x3, Pallas kernels: none -> 61.5 us  [the longest x2 57.9 us: fit(): pl.pallas_call(functools.partial(fit_kernel, first, layers, span // PAIR)...]
    reshape x51 -> x2, local copies, waits for them, and re-layouts: 56.6 us -> 1.05 us  [the longest x1 0.84 us: on_device(): jnp.swapaxes(grad, 0, 1).reshape(epochs, local * PBLK)]
  transfers between devices with their start and end apart: 5 -> 23, of which waited for: 4 -> 13; matrix products, arithmetic and copies ran while one was open for 3% -> 4% of each run, Pallas kernels for 0% -> 3%
where the time goes in v2:
time: 323 us; the launch traced here: 318 us
  waiting for transfers between devices  145 us (45%)
  starting transfers between devices  70.7 us (22%)
  Pallas kernels  61.5 us (19%)
  local copies, waits for them, and re-layouts  19.6 us (6%)
  between operations  14.4 us (4%)
  other arithmetic  5.85 us (2%)
    ppermute x22, waiting for transfers between devices, partner(): lax.ppermute(values, 'tile', [(i, i ^ distance) for i in range(devices)])  145 us
    ppermute x22, starting transfers between devices, partner(): lax.ppermute(values, 'tile', [(i, i ^ distance) for i in range(devices)])  70.7 us
    pallas_call x2, Pallas kernels, fit(): pl.pallas_call(functools.partial(fit_kernel, first, layers, span // PAIR)...  57.9 us
    unnamed x44, local copies, waits for them, and re-layouts  13.4 us
  transfers between devices with their start and end apart: 23, of which 13 were waited for; matrix products, arithmetic and copies ran while one was open for 4% of the time, Pallas kernels for 3%

profile of v2, /device:TPU:0, one launch (start us, length us, event | category | flops | bytes accessed | tf_op | source)
XLA Modules:
  0.0 317.5 jit_solution(1627351762615765055)
XLA Ops:
  7.2 3.0 collective-permute-start.10
  12.0 1.6 copy-done
  16.0 3.6 %pack.1 = (bf16[16,64,256]{2,1,0:T(8,128)(2,1)S(1)}, bf16[16,64,256]{2,1,0:T(8,128)(2,1)S(1)}, bf16[16,64,256]{2,1,0:T(8,128)(2,1)S(1)}, bf16[16,64,256]{2,1,0:T...) custom-call(s32[1]{0:T(128)} %bitcast.here, ...), custom_call_target="tpu_custom_call" | custom-call | tf_op jit(solution)/shard_map/pack/pallas_call | solution.py:76
  22.8 2.6 collective-permute-start.1
  25.6 17.5 %collective-permute-done.refs_8_ = f32[33,8,256]{2,1,0:T(8,128)S(1)} collective-permute-done((f32[33,8,256]{2,1,0:T(8,128)S(1)}, f32[33,8,256]{2,1,0:T(8,128)S(1)}, u32[]{:S(2)}, u32[]{:S(2)}) %collective-permute-start) | collective-permute-done | bytes 270368 | tf_op jit(solution)/shard_map/ppermute | solution.py:284
  43.8 2.1 collective-permute-start.8
  45.9 5.8 %collective-permute-done.2.refs_10_ = f32[33,8,256]{2,1,0:T(8,128)S(1)} collective-permute-done((f32[33,8,256]{2,1,0:T(8,128)S(1)}, f32[33,8,256]{2,1,0:T(8,128)S(1)}, u32[]{:S(2)}, u32[]{:S(2)}) %collective-permute-start.2) | collective-permute-done | bytes 270368 | tf_op jit(solution)/shard_map/ppermute | solution.py:284
  54.4 24.8 %collective-permute-done.7.refs_4_ = bf16[16,64,256]{2,1,0:T(8,128)(2,1)S(1)} collective-permute-done((bf16[16,64,256]{2,1,0:T(8,128)(2,1)S(1)}, bf16[16,64,256]{2,1,0:T(8,128)(2,1)S(1)}, u32[]{:S(2)}, u32[]{:S(2)}) %collective-permute-start.7) | collective-permute-done | bytes 524320 | tf_op jit(solution)/shard_map/ppermute | solution.py:284
  80.0 27.4 %collective-permute-done.8.refs_5_ = bf16[16,64,256]{2,1,0:T(8,128)(2,1)S(1)} collective-permute-done((bf16[16,64,256]{2,1,0:T(8,128)(2,1)S(1)}, bf16[16,64,256]{2,1,0:T(8,128)(2,1)S(1)}, u32[]{:S(2)}, u32[]{:S(2)}) %collective-permute-start.8) | collective-permute-done | bytes 524320 | tf_op jit(solution)/shard_map/ppermute | solution.py:284
  109.1 1.8 collective-permute-start.5
  112.4 4.1 %broadcast_in_dim.2.refs_14_ = f32[128,5,8,256]{3,2,1,0:T(8,128)} broadcast(f32[128,5,256]{2,1,0:T(8,128)} %maximum_bitcast_fusion), dimensions={0,1,3} | broadcast | bytes 5898240 | tf_op jit(solution)/shard_map/broadcast_in_dim | solution.py:367
  119.8 7.5 %fit.2 = (f32[128,64,256]{2,1,0:T(8,128)}, f32[32,64,256]{2,1,0:T(8,128)S(1)}, f32[32,64,256]{2,1,0:T(8,128)S(1)}) custom-call(s32[256]{0:T(256)S(1)} %convert_element_type.38.refs_0_, s32[1536]{0:T(1024)S(1)} %reshape.25.refs_1_, s32[128]{0:T(128)S(1)} %fusion.refs_2_, bf16[16,64,256]{2,1,0:T(8,128)(2,1)S(1)} %copy-done.12, ...), custom_call_target="tpu_custom_call" | custom-call | flops 4294967296 | bytes 41943040 | tf_op jit(solution)/shard_map/fit/pallas_call | solution.py:249
  127.3 25.2 %collective-permute-done.4.refs_5_ = bf16[16,64,256]{2,1,0:T(8,128)(2,1)} collective-permute-done((bf16[16,64,256]{2,1,0:T(8,128)(2,1)}, bf16[16,64,256]{2,1,0:T(8,128)(2,1)}, u32[]{:S(2)}, u32[]{:S(2)}) %collective-permute-start.4) | collective-permute-done | bytes 524320 | tf_op jit(solution)/shard_map/ppermute | solution.py:284
  152.5 50.4 %fit.3 = (f32[64,64,256]{2,1,0:T(8,128)S(1)}, f32[64,64,256]{2,1,0:T(8,128)}, f32[32,64,256]{2,1,0:T(8,128)S(1)}, f32[32,64,256]{2,1,0:T(8,128)S(1)}) custom-call(s32[256]{0:T(256)S(1)} %convert_element_type.38.refs_0_, s32[1536]{0:T(1024)S(1)} %reshape.25.refs_1_, s32[128]{0:T(128)S(1)} %fusion.refs_2_, bf16[16,64,256]{2,1,0:T(8,128)(2,1)S(1)} %copy-done.10, ...), custom_call_target="tpu_custom_call" | custom-call | flops 4294967296 | bytes 41943040 | tf_op jit(solution)/shard_map/fit/pallas_call | solution.py:249
  203.5 9.2 %collective-permute-done.20 = f32[32,64,256]{2,1,0:T(8,128)S(1)} collective-permute-done((f32[32,64,256]{2,1,0:T(8,128)S(1)}, f32[32,64,256]{2,1,0:T(8,128)S(1)}, u32[]{:S(2)}, u32[]{:S(2)}) %collective-permute-start.20) | collective-permute-done | bytes 2097184 | tf_op jit(solution)/shard_map/ppermute | solution.py:284
  213.3 2.2 collective-permute-done.12
  216.9 42.1 %collective-permute-start.16 = (bf16[16,64,256]{2,1,0:T(8,128)(2,1)S(1)}, bf16[16,64,256]{2,1,0:T(8,128)(2,1)S(1)}, u32[]{:S(2)}, u32[]{:S(2)}) collective-permute-start(bf16[16,64,256]{2,1,0:T(8,128)(2,1)S(1)} %get-tuple-element.45), channel_id=1, source_target_pairs={{0,8},{1,9},{2,10},{3,11},{4,12},{5,13},{6,14},{7,15},{8,0},{9,1},... | collective-permute-start | bytes 1572872 | tf_op jit(solution)/shard_map/ppermute | solution.py:284
  259.0 17.8 %collective-permute-done.16 = bf16[16,64,256]{2,1,0:T(8,128)(2,1)S(1)} collective-permute-done((bf16[16,64,256]{2,1,0:T(8,128)(2,1)S(1)}, bf16[16,64,256]{2,1,0:T(8,128)(2,1)S(1)}, u32[]{:S(2)}, u32[]{:S(2)}) %collective-permute-start.16) | collective-permute-done | bytes 524320 | tf_op jit(solution)/shard_map/ppermute | solution.py:284
  277.2 15.1 %collective-permute-start.14 = (bf16[8,64,256]{2,1,0:T(8,128)(2,1)S(1)}, bf16[8,64,256]{2,1,0:T(8,128)(2,1)S(1)}, u32[]{:S(2)}, u32[]{:S(2)}) collective-permute-start(bf16[8,64,256]{2,1,0:T(8,128)(2,1)S(1)} %slice.103), channel_id=1, source_target_pairs={{0,8},{1,9},{2,10},{3,11},{4,12},{5,13},{6,14},{7,15},{8,0},{9,1},... | collective-permute-start | bytes 786440 | tf_op jit(solution)/shard_map/ppermute | solution.py:284
  292.5 2.0 convert_add_fusion
  294.4 4.7 %collective-permute-done.14 = bf16[8,64,256]{2,1,0:T(8,128)(2,1)S(1)} collective-permute-done((bf16[8,64,256]{2,1,0:T(8,128)(2,1)S(1)}, bf16[8,64,256]{2,1,0:T(8,128)(2,1)S(1)}, u32[]{:S(2)}, u32[]{:S(2)}) %collective-permute-start.14) | collective-permute-done | bytes 262176 | tf_op jit(solution)/shard_map/ppermute | solution.py:284
  299.3 5.4 %collective-permute-done.17 = bf16[8,64,256]{2,1,0:T(8,128)(2,1)S(1)} collective-permute-done((bf16[8,64,256]{2,1,0:T(8,128)(2,1)S(1)}, bf16[8,64,256]{2,1,0:T(8,128)(2,1)S(1)}, u32[]{:S(2)}, u32[]{:S(2)}) %collective-permute-start.17) | collective-permute-done | bytes 262176 | tf_op jit(solution)/shard_map/ppermute | solution.py:284
  304.9 1.9 collective-permute-done.15
  306.8 2.9 collective-permute-done.18
  (97 shorter events, 22.7 us)
Async XLA Ops:
  7.2 105.2 %all-gather.2.cloned.1.call-start = ((), (), s32[]{:S(2)}) async-start(), calls=%async_computation | async-start | bytes 4456448 | tf_op jit(solution)/shard_map/all_gather | solution.py:362
  7.2 45.6 %collective-permute-start.10 = (bf16[32,64,256]{2,1,0:T(8,128)(2,1)}, bf16[32,64,256]{2,1,0:T(8,128)(2,1)S(1)}, u32[]{:S(2)}, u32[]{:S(2)}) collective-permute-start(bf16[32,64,256]{2,1,0:T(8,128)(2,1)} %refs_11_.1), channel_id=1, source_target_pairs={{0,2},{1,3},{2,0},{3,1},{4,6},{5,7},{6,4},{7,5},{8,10},{9,11},{10,... | collective-permute-start | bytes 3145736 | tf_op jit(solution)/shard_map/ppermute | solution.py:284
  16.0 94.9 %copy-start.20 = (s32[512,3]{0,1:T(4,128)S(1)}, s32[512,3]{0,1:T(4,128)}, u32[]{:S(2)}) copy-start(s32[512,3]{0,1:T(4,128)} %param.12) | copy-start | bytes 18436
  21.2 21.9 %collective-permute-start = (f32[33,8,256]{2,1,0:T(8,128)S(1)}, f32[33,8,256]{2,1,0:T(8,128)S(1)}, u32[]{:S(2)}, u32[]{:S(2)}) collective-permute-start(f32[33,8,256]{2,1,0:T(8,128)S(1)} %get-tuple-element.22), channel_id=1, source_target_pairs={{0,4},{1,5},{2,6},{3,7},{4,0},{5,1},{6,2},{7,3},{8,12},{9,13},{10,... | collective-permute-start | bytes 811016 | tf_op jit(solution)/shard_map/ppermute | solution.py:284
  22.8 21.1 %collective-permute-start.1 = (f32[33,8,256]{2,1,0:T(8,128)S(1)}, f32[33,8,256]{2,1,0:T(8,128)S(1)}, u32[]{:S(2)}, u32[]{:S(2)}) collective-permute-start(f32[33,8,256]{2,1,0:T(8,128)S(1)} %get-tuple-element.23), channel_id=1, source_target_pairs={{0,8},{1,9},{2,10},{3,11},{4,12},{5,13},{6,14},{7,15},{8,0},{9,1},... | collective-permute-start | bytes 811016 | tf_op jit(solution)/shard_map/ppermute | solution.py:284
  25.4 26.3 %collective-permute-start.2 = (f32[33,8,256]{2,1,0:T(8,128)S(1)}, f32[33,8,256]{2,1,0:T(8,128)S(1)}, u32[]{:S(2)}, u32[]{:S(2)}) collective-permute-start(f32[33,8,256]{2,1,0:T(8,128)S(1)} %get-tuple-element.24), channel_id=1, source_target_pairs={{0,12},{1,13},{2,14},{3,15},{4,8},{5,9},{6,10},{7,11},{8,4},{9,5},... | collective-permute-start | bytes 811016 | tf_op jit(solution)/shard_map/ppermute | solution.py:284
  25.6 126.9 %collective-permute-start.6 = (bf16[32,64,256]{2,1,0:T(8,128)(2,1)}, bf16[32,64,256]{2,1,0:T(8,128)(2,1)}, u32[]{:S(2)}, u32[]{:S(2)}) collective-permute-start(bf16[32,64,256]{2,1,0:T(8,128)(2,1)} %refs_11_.1), channel_id=1, source_target_pairs={{0,1},{1,0},{2,3},{3,2},{4,5},{5,4},{6,7},{7,6},{8,9},{9,8},{10,11... | collective-permute-start | bytes 3145736 | tf_op jit(solution)/shard_map/ppermute | solution.py:284
  43.1 36.2 %collective-permute-start.7 = (bf16[16,64,256]{2,1,0:T(8,128)(2,1)S(1)}, bf16[16,64,256]{2,1,0:T(8,128)(2,1)S(1)}, u32[]{:S(2)}, u32[]{:S(2)}) collective-permute-start(bf16[16,64,256]{2,1,0:T(8,128)(2,1)S(1)} %get-tuple-element.30), channel_id=1, source_target_pairs={{0,4},{1,5},{2,6},{3,7},{4,0},{5,1},{6,2},{7,3},{8,12},{9,13},{10,... | collective-permute-start | bytes 1572872 | tf_op jit(solution)/shard_map/ppermute | solution.py:284
  43.8 63.6 %collective-permute-start.8 = (bf16[16,64,256]{2,1,0:T(8,128)(2,1)S(1)}, bf16[16,64,256]{2,1,0:T(8,128)(2,1)S(1)}, u32[]{:S(2)}, u32[]{:S(2)}) collective-permute-start(bf16[16,64,256]{2,1,0:T(8,128)(2,1)S(1)} %get-tuple-element.31), channel_id=1, source_target_pairs={{0,8},{1,9},{2,10},{3,11},{4,12},{5,13},{6,14},{7,15},{8,0},{9,1},... | collective-permute-start | bytes 1572872 | tf_op jit(solution)/shard_map/ppermute | solution.py:284
  51.7 56.6 %collective-permute-start.9 = (bf16[16,64,256]{2,1,0:T(8,128)(2,1)S(1)}, bf16[16,64,256]{2,1,0:T(8,128)(2,1)S(1)}, u32[]{:S(2)}, u32[]{:S(2)}) collective-permute-start(bf16[16,64,256]{2,1,0:T(8,128)(2,1)S(1)} %get-tuple-element.32), channel_id=1, source_target_pairs={{0,12},{1,13},{2,14},{3,15},{4,8},{5,9},{6,10},{7,11},{8,4},{9,5},... | collective-permute-start | bytes 1572872 | tf_op jit(solution)/shard_map/ppermute | solution.py:284
  52.8 58.6 %collective-permute-start.11 = (bf16[32,64,256]{2,1,0:T(8,128)(2,1)S(1)}, bf16[32,64,256]{2,1,0:T(8,128)(2,1)S(1)}, u32[]{:S(2)}, u32[]{:S(2)}) collective-permute-start(bf16[32,64,256]{2,1,0:T(8,128)(2,1)S(1)} %collective-permute-done.10.refs_11_), channel_id=1, source_target_pairs={{0,1},{1,0},{2,3},{3,2},{4,5},{5,4},{6,7},{7,6},{8,9},{9,8},{10,11... | collective-permute-start | bytes 3145736 | tf_op jit(solution)/shard_map/ppermute | solution.py:284
  80.0 47.3 %collective-permute-start.3 = (bf16[16,64,256]{2,1,0:T(8,128)(2,1)}, bf16[16,64,256]{2,1,0:T(8,128)(2,1)}, u32[]{:S(2)}, u32[]{:S(2)}) collective-permute-start(bf16[16,64,256]{2,1,0:T(8,128)(2,1)} %get-tuple-element.26), channel_id=1, source_target_pairs={{0,4},{1,5},{2,6},{3,7},{4,0},{5,1},{6,2},{7,3},{8,12},{9,13},{10,... | collective-permute-start | bytes 1572872 | tf_op jit(solution)/shard_map/ppermute | solution.py:284
  108.2 44.2 %collective-permute-start.4 = (bf16[16,64,256]{2,1,0:T(8,128)(2,1)}, bf16[16,64,256]{2,1,0:T(8,128)(2,1)}, u32[]{:S(2)}, u32[]{:S(2)}) collective-permute-start(bf16[16,64,256]{2,1,0:T(8,128)(2,1)} %get-tuple-element.27), channel_id=1, source_target_pairs={{0,8},{1,9},{2,10},{3,11},{4,12},{5,13},{6,14},{7,15},{8,0},{9,1},... | collective-permute-start | bytes 1572872 | tf_op jit(solution)/shard_map/ppermute | solution.py:284
  109.1 43.4 %collective-permute-start.5 = (bf16[16,64,256]{2,1,0:T(8,128)(2,1)}, bf16[16,64,256]{2,1,0:T(8,128)(2,1)}, u32[]{:S(2)}, u32[]{:S(2)}) collective-permute-start(bf16[16,64,256]{2,1,0:T(8,128)(2,1)} %get-tuple-element.28), channel_id=1, source_target_pairs={{0,12},{1,13},{2,14},{3,15},{4,8},{5,9},{6,10},{7,11},{8,4},{9,5},... | collective-permute-start | bytes 1572872 | tf_op jit(solution)/shard_map/ppermute | solution.py:284
  202.9 12.6 %collective-permute-start.12 = (f32[64,64,256]{2,1,0:T(8,128)}, f32[64,64,256]{2,1,0:T(8,128)S(1)}, u32[]{:S(2)}, u32[]{:S(2)}) collective-permute-start(f32[64,64,256]{2,1,0:T(8,128)} %get-tuple-element.35), channel_id=1, source_target_pairs={{0,1},{1,0},{2,3},{3,2},{4,5},{5,4},{6,7},{7,6},{8,9},{9,8},{10,11... | collective-permute-start | bytes 12582920 | tf_op jit(solution)/shard_map/ppermute | solution.py:284
  202.9 9.8 %collective-permute-start.20 = (f32[32,64,256]{2,1,0:T(8,128)S(1)}, f32[32,64,256]{2,1,0:T(8,128)S(1)}, u32[]{:S(2)}, u32[]{:S(2)}) collective-permute-start(f32[32,64,256]{2,1,0:T(8,128)S(1)} %get-tuple-element.39), channel_id=1, source_target_pairs={{0,1},{1,0},{2,3},{3,2},{4,5},{5,4},{6,7},{7,6},{8,9},{9,8},{10,11... | collective-permute-start | bytes 6291464 | tf_op jit(solution)/shard_map/ppermute | solution.py:284
  203.4 89.0 %collective-permute-start.19 = (f32[32,64,256]{2,1,0:T(8,128)S(1)}, f32[32,64,256]{2,1,0:T(8,128)S(1)}, u32[]{:S(2)}, u32[]{:S(2)}) collective-permute-start(f32[32,64,256]{2,1,0:T(8,128)S(1)} %get-tuple-element.37), channel_id=1, source_target_pairs={{0,1},{1,0},{2,3},{3,2},{4,5},{5,4},{6,7},{7,6},{8,9},{9,8},{10,11... | collective-permute-start | bytes 6291464 | tf_op jit(solution)/shard_map/ppermute | solution.py:284
  213.2 79.2 %collective-permute-start.21 = (bf16[32,64,256]{2,1,0:T(8,128)(2,1)S(1)}, bf16[32,64,256]{2,1,0:T(8,128)(2,1)S(1)}, u32[]{:S(2)}, u32[]{:S(2)}) collective-permute-start(bf16[32,64,256]{2,1,0:T(8,128)(2,1)S(1)} %add_convert_fusion), channel_id=1, source_target_pairs={{0,2},{1,3},{2,0},{3,1},{4,6},{5,7},{6,4},{7,5},{8,10},{9,11},{10,... | collective-permute-start | bytes 3145736 | tf_op jit(solution)/shard_map/ppermute | solution.py:284
  216.9 42.2 %collective-permute-start.13 = (bf16[16,64,256]{2,1,0:T(8,128)(2,1)S(1)}, bf16[16,64,256]{2,1,0:T(8,128)(2,1)S(1)}, u32[]{:S(2)}, u32[]{:S(2)}) collective-permute-start(bf16[16,64,256]{2,1,0:T(8,128)(2,1)S(1)} %get-tuple-element.44), channel_id=1, source_target_pairs={{0,2},{1,3},{2,0},{3,1},{4,6},{5,7},{6,4},{7,5},{8,10},{9,11},{10,... | collective-permute-start | bytes 1572872 | tf_op jit(solution)/shard_map/ppermute | solution.py:284
  216.9 59.9 %collective-permute-start.16 = (bf16[16,64,256]{2,1,0:T(8,128)(2,1)S(1)}, bf16[16,64,256]{2,1,0:T(8,128)(2,1)S(1)}, u32[]{:S(2)}, u32[]{:S(2)}) collective-permute-start(bf16[16,64,256]{2,1,0:T(8,128)(2,1)S(1)} %get-tuple-element.45), channel_id=1, source_target_pairs={{0,8},{1,9},{2,10},{3,11},{4,12},{5,13},{6,14},{7,15},{8,0},{9,1},... | collective-permute-start | bytes 1572872 | tf_op jit(solution)/shard_map/ppermute | solution.py:284
  277.2 21.9 %collective-permute-start.14 = (bf16[8,64,256]{2,1,0:T(8,128)(2,1)S(1)}, bf16[8,64,256]{2,1,0:T(8,128)(2,1)S(1)}, u32[]{:S(2)}, u32[]{:S(2)}) collective-permute-start(bf16[8,64,256]{2,1,0:T(8,128)(2,1)S(1)} %slice.103), channel_id=1, source_target_pairs={{0,8},{1,9},{2,10},{3,11},{4,12},{5,13},{6,14},{7,15},{8,0},{9,1},... | collective-permute-start | bytes 786440 | tf_op jit(solution)/shard_map/ppermute | solution.py:284
  292.4 12.3 %collective-permute-start.17 = (bf16[8,64,256]{2,1,0:T(8,128)(2,1)S(1)}, bf16[8,64,256]{2,1,0:T(8,128)(2,1)S(1)}, u32[]{:S(2)}, u32[]{:S(2)}) collective-permute-start(bf16[8,64,256]{2,1,0:T(8,128)(2,1)S(1)} %slice.102), channel_id=1, source_target_pairs={{0,4},{1,5},{2,6},{3,7},{4,0},{5,1},{6,2},{7,3},{8,12},{9,13},{10,... | collective-permute-start | bytes 786440 | tf_op jit(solution)/shard_map/ppermute | solution.py:284
  299.2 7.6 %collective-permute-start.15 = (bf16[4,64,256]{2,1,0:T(8,128)(2,1)S(1)}, bf16[4,64,256]{2,1,0:T(8,128)(2,1)S(1)}, u32[]{:S(2)}, u32[]{:S(2)}) collective-permute-start(bf16[4,64,256]{2,1,0:T(8,128)(2,1)S(1)} %slice.105), channel_id=1, source_target_pairs={{0,4},{1,5},{2,6},{3,7},{4,0},{5,1},{6,2},{7,3},{8,12},{9,13},{10,... | collective-permute-start | bytes 393224 | tf_op jit(solution)/shard_map/ppermute | solution.py:284
  304.7 5.0 %collective-permute-start.18 = (bf16[4,64,256]{2,1,0:T(8,128)(2,1)S(1)}, bf16[4,64,256]{2,1,0:T(8,128)(2,1)S(1)}, u32[]{:S(2)}, u32[]{:S(2)}) collective-permute-start(bf16[4,64,256]{2,1,0:T(8,128)(2,1)S(1)} %slice.104), channel_id=1, source_target_pairs={{0,2},{1,3},{2,0},{3,1},{4,6},{5,7},{6,4},{7,5},{8,10},{9,11},{10,... | collective-permute-start | bytes 393224 | tf_op jit(solution)/shard_map/ppermute | solution.py:284
  (20 other events, 157.9 us)
Sparse Core Ops, SparseCore 0:
  12.1 96.0 all-gather.1
